TPU v7x, 32 devices: a whole 2x2x4 slice. The times are simulated.
32 devices in a mesh: energy: 8 (over z, y), col: 4 (over x, core).
Axes of the slice: x: 2, y: 2, z: 4, core: 2. Of those that a mesh axis runs over, the one named last changes fastest.
Arguments:
- lesser: float32 [128, 2, 12, 1152], P('energy', None, 'col'), may hold values from -6 to 6
- greater_transposed: float32 [128, 2, 12, 1152], P('energy', None, 'col'), may hold values from -6 to 6
- coulomb: bfloat16 [1152, 1152], P('energy', 'col'), may hold values from -0.1875 to 0.1875
Outputs:
- screened: float32 [128, 2, 12, 1152], P('energy', None, 'col')
All inputs are finite; a program needn't handle non-finite values.
Results may differ from a plain program's by a relative error of at most 0.0029.
Values may be sent and summed in bfloat16 or wider, within the bound.
A program may use at most 64 MiB of HBM per device.

v0:
```python
import math

import jax
import jax.numpy as jnp
from jax import lax
from jax.sharding import PartitionSpec as P


def product(left, right):
    return jnp.dot(left, right, precision=lax.Precision.HIGHEST, preferred_element_type=jnp.float32)


def per_device(lesser, greater_transposed, coulomb):
    lesser_all, greater_all = (
        lax.all_to_all(lesser, "energy", split_axis=3, concat_axis=0, tiled=True),
        lax.all_to_all(greater_transposed, "energy", split_axis=3, concat_axis=0, tiled=True),
    )
    energies = lesser_all.shape[0]
    columns_here = lesser_all.shape[2]
    rows_here = lesser_all.shape[3]
    padded = 2 * energies
    lesser_re = lesser_all[:, 0].reshape(energies, -1)
    lesser_im = lesser_all[:, 1].reshape(energies, -1)
    greater_re = greater_all[:, 0].reshape(energies, -1)
    greater_im = greater_all[:, 1].reshape(energies, -1)
    frequency = lax.broadcasted_iota(jnp.int32, (padded, energies), 0)
    position = lax.broadcasted_iota(jnp.int32, (padded, energies), 1)
    phases = frequency * position % padded
    angles = phases.astype(jnp.float32) * (2.0 * math.pi / padded)
    cos_table = jnp.cos(angles)
    sin_table = jnp.sin(angles)
    left_re = product(cos_table, lesser_re) + product(sin_table, lesser_im)
    left_im = product(cos_table, lesser_im) - product(sin_table, lesser_re)
    right_re = product(cos_table, greater_re) - product(sin_table, greater_im)
    right_im = product(cos_table, greater_im) + product(sin_table, greater_re)
    mixed_re = left_re * right_re - left_im * right_im
    mixed_im = left_re * right_im + left_im * right_re
    corr_re = (product(cos_table.T, mixed_re) - product(sin_table.T, mixed_im)) / padded
    corr_im = (product(cos_table.T, mixed_im) + product(sin_table.T, mixed_re)) / padded
    factor = 1.0 / math.sqrt(energies)
    polar_re = (corr_im * factor).reshape(energies, columns_here, rows_here)
    polar_im = (-corr_re * factor).reshape(energies, columns_here, rows_here)
    polarized = jnp.stack([polar_re, polar_im], axis=1).astype(jnp.bfloat16)
    coulomb_wide = lax.all_gather(coulomb, "col", axis=1, tiled=True)
    order = coulomb_wide.shape[1]
    returned = lax.all_to_all(polarized, "energy", split_axis=0, concat_axis=3, tiled=True)
    flattened = returned.reshape(-1, order)
    running = jnp.dot(
        flattened,
        lax.all_gather(coulomb_wide, "energy", axis=0, tiled=True),
        preferred_element_type=jnp.float32,
    )
    screened = running.reshape(returned.shape)
    return screened


def solution(mesh):
    placed = (P("energy", None, "col", None), P("energy", None, "col", None), P("energy", "col"))
    return jax.shard_map(
        per_device,
        mesh=mesh,
        in_specs=placed,
        out_specs=P("energy", None, "col", None),
        check_vma=False,
    )
```

profile of v0, /device:TPU:0, one launch (start us, length us, event | category | flops | bytes accessed | tf_op | source)
XLA Modules:
  0.0 122.8 jit_solution(10056228635309748826)
XLA Ops:
  6.5 4.7 %copy.36 = f32[16,2,3,1152]{0,1,2,3:T(2,128)S(1)} copy(f32[16,2,3,1152]{3,1,2,0:T(2,128)} %param.4) | data formatting | bytes 884736 | tf_op args[1]
  11.2 5.5 %reshape.10 = f32[8,1,13824]{2,1,0:T(1,128)} reshape(f32[1152,3,2,16]{3,2,1,0:T(2,128)S(1)} %bitcast.51) | data formatting | bytes 884736
  16.6 7.3 %all-to-all-start.1 = ((f32[8,1,13824]{2,1,0:T(1,128)}), f32[8,1,13824]{2,1,0:T(1,128)}, u32[]{:S(2)}, u32[]{:S(2)}) async-start(f32[8,1,13824]{2,1,0:T(1,128)} %reshape.10), calls=%async_computation.1 | async-start | bytes 884736 | tf_op jit(solution)/shard_map/all_to_all | solution.py:16
  24.0 6.9 %all-gather = bf16[4,288,144]{1,2,0:T(8,128)(2,1)S(1)} all-gather(bf16[1,288,144]{1,2,0:T(8,128)(2,1)} %bitcast.67), channel_id=1, replica_groups=mesh['energy'=8,'col'=4] {'col'}, dimensions={0}, use_global_device_ids=true | all-gather | bytes 414720 | tf_op jit(solution)/shard_map/all_gather | solution.py:44
  31.1 1.0 reshape.6
  32.2 4.7 %copy.32 = f32[16,2,3,1152]{0,1,2,3:T(2,128)S(1)} copy(f32[16,2,3,1152]{3,1,2,0:T(2,128)} %param.3) | data formatting | bytes 884736 | tf_op args[0]
  36.8 5.4 %reshape.8 = f32[8,1,13824]{2,1,0:T(1,128)} reshape(f32[1152,3,2,16]{3,2,1,0:T(2,128)S(1)} %bitcast.52) | data formatting | bytes 884736
  42.3 5.9 %all-to-all-start = ((f32[8,1,13824]{2,1,0:T(1,128)}), f32[8,1,13824]{2,1,0:T(1,128)}, u32[]{:S(2)}, u32[]{:S(2)}) async-start(f32[8,1,13824]{2,1,0:T(1,128)} %reshape.8), calls=%async_computation | async-start | bytes 884736 | tf_op jit(solution)/shard_map/all_to_all | solution.py:15
  48.8 3.5 %reduce = f32[8,13824]{1,0:T(8,128)} reduce(f32[8,1,13824]{2,1,0:T(1,128)} %all-to-all-done.1, f32[]{:T(128)} %broadcast.39), dimensions={1}, to_apply=%all_to_all.41.reduce_sub_computation | reduce | bytes 884740 | tf_op jit(solution)/shard_map/all_to_all | solution.py:16
  52.3 5.8 %reshape.11 = f32[1152,3,2,16]{3,2,1,0:T(2,128)S(1)} reshape(f32[8,13824]{1,0:T(8,128)} %reduce) | data formatting | bytes 884736
  58.1 4.1 %copy.37 = f32[16,2,3,8,144]{4,0,3,2,1:T(8,128)} copy(f32[16,2,3,8,144]{0,1,2,4,3:T(2,128)S(1)} %bitcast.49) | data formatting | bytes 884736 | tf_op jit(solution)/shard_map/all_to_all | solution.py:16
  62.2 1.2 fusion.82
  65.1 1.0 all-to-all-done
  66.0 3.5 %reduce.1 = f32[8,13824]{1,0:T(8,128)} reduce(f32[8,1,13824]{2,1,0:T(1,128)} %all-to-all-done, f32[]{:T(128)} %broadcast.39), dimensions={1}, to_apply=%all_to_all.37.reduce_sub_computation | reduce | bytes 884740 | tf_op jit(solution)/shard_map/all_to_all | solution.py:15
  69.5 5.8 %reshape.9 = f32[1152,3,2,16]{3,2,1,0:T(2,128)S(1)} reshape(f32[8,13824]{1,0:T(8,128)} %reduce.1) | data formatting | bytes 884736
  75.3 4.0 %copy.33 = f32[16,2,3,8,144]{4,0,3,2,1:T(8,128)} copy(f32[16,2,3,8,144]{0,1,2,4,3:T(2,128)S(1)} %bitcast.50) | data formatting | bytes 884736 | tf_op jit(solution)/shard_map/all_to_all | solution.py:15
  79.3 1.2 fusion.83
  80.9 1.9 %fusion.24 = f32[256,432]{0,1:T(8,128)S(1)} fusion(f32[128,432]{0,1:T(8,128)} %bitcast.57), kind=kOutput, calls=%fused_computation.32 | convolution fusion | flops 170328064 | bytes 663552 | tf_op jit(solution)/shard_map/dot_general | solution.py:10
  82.8 1.0 fusion.26
  83.9 1.0 fusion.20
  84.9 1.0 fusion.22
  85.9 1.0 convolution_add_fusion
  86.9 1.0 convolution_add_fusion.1
  88.0 1.0 convolution_subtract_fusion
  89.0 1.1 multiply_add_fusion
  90.1 1.0 fusion.18
  91.1 1.0 fusion.16
  92.1 1.0 fusion.7
  93.1 1.3 %fusion.6 = bf16[128,432]{0,1:T(8,128)(2,1)S(1)} fusion(f32[128,432]{0,1:T(8,128)S(1)} %fusion.16, f32[256,432]{0,1:T(8,128)S(1)} %get-tuple-element.5), kind=kOutput, calls=%fused_computation.12 | convolution fusion | flops 170604544 | bytes 774144 | tf_op jit(solution)/shard_map/dot_general | solution.py:10
  95.2 16.9 %all_to_all.51 = bf16[128,2,3,144]{3,1,2,0:T(2,128)(2,1)S(1)} all-to-all(bf16[128,2,3,144]{3,1,2,0:T(2,128)(2,1)S(1)} %copy.40), channel_id=1, replica_groups=mesh['energy'=8,'col'=4] {'energy'}, dimensions={0} | all-to-all | bytes 442368 | tf_op jit(solution)/shard_map/all_to_all | solution.py:46
  112.6 2.3 %fusion = f32[16,2,3,1152]{3,0,2,1:T(8,128)S(1)} fusion(bf16[16,2,3,1152]{3,0,2,1:T(8,128)(2,1)S(1)} %dot_general.53, bf16[1152,1152]{1,0:T(8,128)(2,1)} %all-gather.3.cloned.1.call-done), kind=kOutput, calls=%fused_computation | convolution fusion | flops 254803968 | bytes 3317760 | tf_op jit(solution)/shard_map/dot_general | solution.py:48
  115.0 1.0 copy.44
  (19 shorter events, 4.1 us)
Async XLA Ops:
  16.6 25.6 %all-to-all-start.1 = ((f32[8,1,13824]{2,1,0:T(1,128)}), f32[8,1,13824]{2,1,0:T(1,128)}, u32[]{:S(2)}, u32[]{:S(2)}) async-start(f32[8,1,13824]{2,1,0:T(1,128)} %reshape.10), calls=%async_computation.1 | async-start | bytes 884736 | tf_op jit(solution)/shard_map/all_to_all | solution.py:16
  23.9 88.7 %all-gather.3.cloned.1.call-start = ((), (), s32[]{:S(2)}) async-start(), calls=%async_computation.3 | async-start | bytes 2985984 | tf_op jit(solution)/shard_map/all_gather | solution.py:50
  42.3 23.7 %all-to-all-start = ((f32[8,1,13824]{2,1,0:T(1,128)}), f32[8,1,13824]{2,1,0:T(1,128)}, u32[]{:S(2)}, u32[]{:S(2)}) async-start(f32[8,1,13824]{2,1,0:T(1,128)} %reshape.8), calls=%async_computation | async-start | bytes 884736 | tf_op jit(solution)/shard_map/all_to_all | solution.py:15
  79.3 4.5 %copy-start.1 = (f32[128,1,3,144]{0,3,2,1:T(8,128)S(1)}, f32[128,1,3,144]{0,3,2,1:T(8,128)}, u32[]{:S(2)}) copy-start(f32[128,1,3,144]{0,3,2,1:T(8,128)} %copy.39) | copy-start | bytes 663556
  79.3 8.6 %copy-start = (f32[128,1,3,144]{0,3,2,1:T(8,128)S(1)}, f32[128,1,3,144]{0,3,2,1:T(8,128)}, u32[]{:S(2)}) copy-start(f32[128,1,3,144]{0,3,2,1:T(8,128)} %copy.38) | copy-start | bytes 663556
Sparse Core Ops, SparseCore 0:
  32.3 62.9 all-gather.2
where the time goes:
time: 124 us; the launch traced here: 123 us
  local copies, waits for them, and re-layouts  48.3 us (39%)
  blocking collectives  23.8 us (19%)
  matrix products  15.8 us (13%)
  between operations  13.6 us (11%)
  starting transfers between devices  13.3 us (11%)
  other arithmetic  7.05 us (6%)
    unnamed x11, local copies, waits for them, and re-layouts  32.8 us
    all_to_all x1, blocking collectives, per_device(): lax.all_to_all(polarized, 'energy', split_axis=0, concat_axis=3, tiled=True)  16.9 us
    dot_general x12, matrix products, product(): jnp.dot(left, right, precision=lax.Precision.HIGHEST, preferred_element_t...  13.4 us
    all_to_all x1, starting transfers between devices, per_device(): lax.all_to_all(greater_transposed, 'energy', split_axis=3, concat_axis=0,...  7.28 us
    all_gather x1, blocking collectives, per_device(): coulomb_wide = lax.all_gather(coulomb, 'col', axis=1, tiled=True)  6.94 us
    all_to_all x1, starting transfers between devices, per_device(): lax.all_to_all(lesser, 'energy', split_axis=3, concat_axis=0, tiled=True)  5.94 us
    all_to_all x2, local copies, waits for them, and re-layouts, per_device(): lax.all_to_all(greater_transposed, 'energy', split_axis=3, concat_axis=0,...  4.68 us
    all_to_all x1, local copies, waits for them, and re-layouts, per_device(): lax.all_to_all(lesser, 'energy', split_axis=3, concat_axis=0, tiled=True)  4.03 us
  transfers between devices with their start and end apart: 3, of which 1 were waited for; matrix products, arithmetic and copies ran while one was open for 47% of the time, Pallas kernels for 0%

commit v1 on v0

--- a/solution.py
+++ b/solution.py
@@ -1,9 +1,18 @@
+import functools
 import math
 
 import jax
 import jax.numpy as jnp
+import ml_dtypes
+import numpy as np
 from jax import lax
+from jax.experimental import pallas as pl
+from jax.experimental.pallas import tpu as pltpu
 from jax.sharding import PartitionSpec as P
+
+LANES = 128
+REST = 32
+MESH = pl.DeviceIdType.MESH
 
 
 def product(left, right):
@@ -54,10 +63,282 @@
     return screened
 
 
+def split_table(table):
+    high = table.astype(ml_dtypes.bfloat16)
+    low = (table - high.astype(np.float64)).astype(ml_dtypes.bfloat16)
+    return np.concatenate([high, high, low], axis=1)
+
+
+def tables(energies):
+    padded = 2 * energies
+    angle = 2.0 * math.pi / padded * (np.outer(np.arange(padded), np.arange(energies)) % padded)
+    cos, sin = np.cos(angle), np.sin(angle)
+    forward_re = np.stack([cos, sin], axis=2).reshape(padded, padded)
+    forward_im = np.stack([-sin, cos], axis=2).reshape(padded, padded)
+    forward = np.concatenate([forward_re, forward_im], axis=0)
+    scale = 1.0 / (padded * math.sqrt(energies))
+    corr_re = np.concatenate([cos.T, -sin.T], axis=1)
+    corr_im = np.concatenate([sin.T, cos.T], axis=1)
+    inverse = np.stack([corr_im, -corr_re], axis=1).reshape(padded, 2 * padded) * scale
+    return split_table(forward), split_table(inverse)
+
+
+def high_low(x):
+    high = x.astype(jnp.bfloat16)
+    return high, (x - high.astype(jnp.float32)).astype(jnp.bfloat16)
+
+
+def kernel(n, m, l_ref, r_ref, w_ref, tf_ref, ti_ref, o_ref, give, take, polar, panel, coul,
+           lr_send, lr_recv, p_send, p_recv, c_send, c_recv, own_sem):
+    here_e, here_c = lax.axis_index("energy"), lax.axis_index("col")
+    block, cols, _, order = l_ref.shape
+    tiles_k = order // LANES
+    total = cols * tiles_k
+    full, extra = total // n, total % n
+    slots = full + (1 if extra else 0)
+    rows = 2 * block
+    depth, width = w_ref.shape
+    wide = width - REST
+    groups = LANES // REST
+    third = depth // 3
+
+    z, y = here_e // 2, lax.rem(here_e, 2)
+    x, core = here_c // 2, lax.rem(here_c, 2)
+    nz = n // 2
+
+    def at_e(s, b):
+        return lax.rem(z + nz - s, nz) * 2 + (y if b == 0 else 1 - y)
+
+    def at_c(a):
+        return (x if a == 0 else 1 - x) * 2 + core
+
+    peer_y = z * 2 + 1 - y
+    peer_x = (1 - x) * 2 + core
+    peer_core = x * 2 + 1 - core
+
+    barrier = pltpu.get_barrier_semaphore()
+    for s in range(1, n):
+        pl.semaphore_signal(barrier, inc=1, device_id={"energy": lax.rem(here_e + s, n)}, device_id_type=MESH)
+    for peer in (peer_x, peer_core):
+        pl.semaphore_signal(barrier, inc=1, device_id={"col": peer}, device_id_type=MESH)
+
+    sign = jnp.where(lax.broadcasted_iota(jnp.int32, (rows, LANES), 0) % 2 == 0, 1.0, -1.0)
+    for t in range(slots * n):
+        j, d = t // n, t % n
+        if t >= total:
+            continue
+        c, k = t // tiles_k, t % tiles_k
+        lanes = slice(k * LANES, (k + 1) * LANES)
+        high, low = high_low(l_ref[:, c, :, lanes].reshape(rows, LANES))
+        give[d, j, 0:rows] = high
+        give[d, j, rows:2 * rows] = low
+        right = r_ref[:, c, :, lanes].reshape(rows, LANES) * sign
+        give[d, j, 2 * rows:3 * rows] = right.astype(jnp.bfloat16)
+
+    pl.semaphore_wait(barrier, n - 1 + 2)
+
+    sends = []
+
+    def parts(source, target, sems_s, sems_r, s, dev, has_extra):
+        if full:
+            cp = pltpu.make_async_remote_copy(
+                src_ref=source(0, full), dst_ref=target(0, full), send_sem=sems_s.at[0, s],
+                recv_sem=sems_r.at[0, s], device_id={"energy": dev}, device_id_type=MESH)
+            cp.start()
+            sends.append((cp, None))
+        if extra:
+            cq = pltpu.make_async_remote_copy(
+                src_ref=source(full, 1), dst_ref=target(full, 1), send_sem=sems_s.at[1, s],
+                recv_sem=sems_r.at[1, s], device_id={"energy": dev}, device_id_type=MESH)
+            pl.when(has_extra)(cq.start)
+            sends.append((cq, has_extra))
+
+    for s in range(1, n):
+        dev = lax.rem(here_e + s, n)
+        parts(lambda a, w: give.at[dev, pl.ds(a, w)], lambda a, w: take.at[pl.ds(a, w), here_e],
+              lr_send, lr_recv, s, dev, dev < extra)
+    own = pltpu.make_async_copy(give.at[here_e], take.at[:, here_e], own_sem.at[0])
+    own.start()
+
+    w = w_ref[...]
+    coul[here_e, here_c, 0:depth] = w[:, 0:LANES]
+    coul[here_e, here_c, depth:2 * depth] = w[:, LANES:2 * LANES]
+    rest = w[:, wide:].astype(jnp.float32)
+    packed = jnp.concatenate(
+        [rest[q * third:(q + 1) * third] for q in range(3)] + [jnp.zeros((third, LANES - 3 * REST), jnp.float32)],
+        axis=1)
+    coul[here_e, here_c, 2 * depth:2 * depth + third] = packed.astype(jnp.bfloat16)
+
+    got = {}
+
+    def share(index, e, c, dev):
+        cp = pltpu.make_async_remote_copy(
+            src_ref=coul.at[e, c], dst_ref=coul.at[e, c], send_sem=c_send.at[index],
+            recv_sem=c_recv.at[index], device_id=dev, device_id_type=MESH)
+        cp.start()
+        sends.append((cp, None))
+        got[index] = cp
+
+    iz, iy, ix, ic = 0, nz, 2 * nz, 4 * nz
+    for s in range(1, nz):
+        share(iz + s, here_e, here_c, {"energy": lax.rem(z + s, nz) * 2 + y})
+    share(iy, here_e, here_c, {"energy": peer_y})
+    share(ix, here_e, here_c, {"col": peer_x})
+    share(ic, here_e, here_c, {"col": peer_core})
+    for s in range(1, nz):
+        got[iz + s].wait_recv()
+        e = at_e(s, 0)
+        share(iy + s, e, here_c, {"energy": peer_y})
+        share(ix + 2 * s, e, here_c, {"col": peer_x})
+        share(ic + 4 * s, e, here_c, {"col": peer_core})
+    for s in range(nz):
+        got[iy + s].wait_recv()
+        e = at_e(s, 1)
+        share(ix + 2 * s + 1, e, here_c, {"col": peer_x})
+        share(ic + 4 * s + 2, e, here_c, {"col": peer_core})
+
+    def arrive(source, target, sems_s, sems_r, s):
+        dev = lax.rem(here_e + s, n)
+        if full:
+            pltpu.make_async_remote_copy(
+                src_ref=source(0, full), dst_ref=target(0, full), send_sem=sems_s.at[0, s],
+                recv_sem=sems_r.at[0, s], device_id={"energy": dev}, device_id_type=MESH).wait_recv()
+
+    def arrive_extra(source, target, sems_s, sems_r, s, has):
+        dev = lax.rem(here_e + s, n)
+        if extra:
+            pl.when(has)(pltpu.make_async_remote_copy(
+                src_ref=source(full, 1), dst_ref=target(full, 1), send_sem=sems_s.at[1, s],
+                recv_sem=sems_r.at[1, s], device_id={"energy": dev}, device_id_type=MESH).wait_recv)
+
+    own.wait()
+    for s in range(1, n):
+        src, dst = (lambda a, w: give.at[0, pl.ds(a, w)]), (lambda a, w: take.at[pl.ds(a, w), 0])
+        arrive(src, dst, lr_send, lr_recv, s)
+        arrive_extra(src, dst, lr_send, lr_recv, s, here_e < extra)
+
+    def piece(i):
+        return jnp.concatenate(
+            [take[j, :, i * rows:(i + 1) * rows].reshape(n * rows, LANES) for j in range(slots)], axis=1)
+
+    l_high, l_low, r_high = piece(0), piece(1), piece(2)
+    span = n * rows
+    left = jnp.dot(tf_ref[...], jnp.concatenate([l_high, l_low, l_high], axis=0),
+                   preferred_element_type=jnp.float32)
+    right = jnp.dot(tf_ref[:, span:], jnp.concatenate([r_high, r_high], axis=0),
+                    preferred_element_type=jnp.float32)
+    a, b = left[:span], left[span:]
+    c, d = right[:span], right[span:]
+    mixed = jnp.concatenate([a * c + b * d, b * c - a * d], axis=0)
+    m_high, m_low = high_low(mixed)
+    polarized = jnp.dot(ti_ref[...], jnp.concatenate([m_high, m_low, m_high], axis=0),
+                        preferred_element_type=jnp.float32).astype(jnp.bfloat16)
+    for j in range(slots):
+        polar[j] = polarized[:, j * LANES:(j + 1) * LANES].reshape(n, rows, LANES)
+
+    for s in range(1, n):
+        dev = lax.rem(here_e + s, n)
+        parts(lambda a, w: polar.at[pl.ds(a, w), dev], lambda a, w: panel.at[pl.ds(a, w), here_e],
+              p_send, p_recv, s, dev, here_e < extra)
+    own_p = pltpu.make_async_copy(polar.at[:, here_e], panel.at[:, here_e], own_sem.at[1])
+    own_p.start()
+
+    for s in range(nz):
+        for b in range(2):
+            got[ix + 2 * s + b].wait_recv()
+            share(ic + 4 * s + 2 * b + 1, at_e(s, b), at_c(1), {"col": peer_core})
+    for i in range(4 * nz):
+        got[ic + i].wait_recv()
+
+    lane = lax.broadcasted_iota(jnp.int32, (third, LANES), 1)
+    rests = []
+    for g in range(n):
+        for q in range(3):
+            acc = jnp.zeros((third, LANES), jnp.float32)
+            for cc in range(m):
+                u = coul[g, cc, 2 * depth:2 * depth + third].astype(jnp.float32)
+                shift = (cc - q) * REST % LANES
+                if shift:
+                    u = pltpu.roll(u, shift, 1)
+                acc = jnp.where((lane >= cc * REST) & (lane < (cc + 1) * REST), u, acc)
+            rests.append(acc.astype(jnp.bfloat16))
+    rest_all = jnp.concatenate(rests, axis=0)
+
+    own_p.wait()
+    for s in range(1, n):
+        src, dst = (lambda a, w: polar.at[pl.ds(a, w), 0]), (lambda a, w: panel.at[pl.ds(a, w), 0])
+        arrive(src, dst, p_send, p_recv, s)
+        arrive_extra(src, dst, p_send, p_recv, s, lax.rem(here_e + n - s, n) < extra)
+
+    flat = jnp.concatenate(
+        [jnp.concatenate([panel[t // n, t % n] for t in range(c * tiles_k, (c + 1) * tiles_k)], axis=1)
+         for c in range(cols)], axis=0)
+    rest_out = jnp.dot(flat, rest_all, preferred_element_type=jnp.float32)
+    pieces = []
+    for cc in range(m):
+        weight = jnp.concatenate(
+            [coul[:, cc, h * depth:(h + 1) * depth].reshape(n * depth, LANES) for h in range(2)], axis=1)
+        pieces.append(jnp.dot(flat, weight, preferred_element_type=jnp.float32))
+        pieces.append(rest_out[:, cc * REST:(cc + 1) * REST])
+    o_ref[...] = jnp.concatenate(pieces, axis=1)
+
+    for cp, cond in sends:
+        if cond is None:
+            cp.wait_send()
+        else:
+            pl.when(cond)(cp.wait_send)
+
+
+def fused(n, m, lesser, greater_transposed, coulomb):
+    block, _, cols, order = lesser.shape
+    depth, width = coulomb.shape
+    energies = n * block
+    total = cols * order // LANES
+    slots = -(-total // n)
+    rows = 2 * block
+    forward, inverse = tables(energies)
+    vmem = pl.BlockSpec(memory_space=pltpu.VMEM)
+    out = pl.pallas_call(
+        functools.partial(kernel, n, m),
+        out_shape=jax.ShapeDtypeStruct((cols * rows, order), jnp.float32),
+        in_specs=[vmem] * 5,
+        out_specs=vmem,
+        scratch_shapes=[
+            pltpu.VMEM((n, slots, 3 * rows, LANES), jnp.bfloat16),
+            pltpu.VMEM((slots, n, 3 * rows, LANES), jnp.bfloat16),
+            pltpu.VMEM((slots, n, rows, LANES), jnp.bfloat16),
+            pltpu.VMEM((slots, n, rows, LANES), jnp.bfloat16),
+            pltpu.VMEM((n, m, 2 * depth + depth // 3, LANES), jnp.bfloat16),
+            pltpu.SemaphoreType.DMA((2, n)),
+            pltpu.SemaphoreType.DMA((2, n)),
+            pltpu.SemaphoreType.DMA((2, n)),
+            pltpu.SemaphoreType.DMA((2, n)),
+            pltpu.SemaphoreType.DMA((n * m,)),
+            pltpu.SemaphoreType.DMA((n * m,)),
+            pltpu.SemaphoreType.DMA((2,)),
+        ],
+        compiler_params=pltpu.CompilerParams(
+            collective_id=0, has_side_effects=True, vmem_limit_bytes=40 * 2**20),
+        cost_estimate=pl.CostEstimate(flops=2_000_000_000, bytes_accessed=8_000_000, transcendentals=0),
+    )(lesser.transpose(0, 2, 1, 3), greater_transposed.transpose(0, 2, 1, 3), coulomb,
+      jnp.asarray(forward), jnp.asarray(inverse))
+    return out.reshape(cols, block, 2, order).transpose(1, 2, 0, 3)
+
+
 def solution(mesh):
     placed = (P("energy", None, "col", None), P("energy", None, "col", None), P("energy", "col"))
+    n, m = mesh.shape["energy"], mesh.shape["col"]
+
+    def local(lesser, greater_transposed, coulomb):
+        depth, width = coulomb.shape
+        fits = (m == 4 and n % 2 == 0 and depth % 48 == 0 and width == 2 * LANES + REST
+                and lesser.shape[0] % 8 == 0 and lesser.shape[3] % LANES == 0)
+        if fits:
+            return fused(n, m, lesser, greater_transposed, coulomb)
+        return per_device(lesser, greater_transposed, coulomb)
+
     return jax.shard_map(
-        per_device,
+        local,
         mesh=mesh,
         in_specs=placed,
         out_specs=P("energy", None, "col", None),

time: 124 us -> 51.5 us (0.42)
  the two profiles are of different devices: /device:TPU:0 before, /device:TPU:1 now
where the time goes in v1:
time: 51.5 us; the launch traced here: 51.2 us
  Pallas kernels  44.9 us (87%)
  local copies, waits for them, and re-layouts  6.25 us (12%)
    pallas_call x1, Pallas kernels, fused(): pl.pallas_call(functools.partial(kernel, n, m), out_shape=jax.ShapeDtypeS...  44.9 us
    unnamed x10, local copies, waits for them, and re-layouts  5.19 us
    reshape x2, local copies, waits for them, and re-layouts, fused(): return out.reshape(cols, block, 2, order).transpose(1, 2, 0, 3)  1.06 us

profile of v1, /device:TPU:1, one launch (start us, length us, event | category | flops | bytes accessed | tf_op | source)
XLA Modules:
  0.0 51.2 jit_solution(14402673681271267182)
XLA Ops:
  0.0 0.0 copy-start
  0.0 1.0 %copy-done = f32[16,2,3,1152]{3,1,2,0:T(2,128)S(1)} copy-done((f32[16,2,3,1152]{3,1,2,0:T(2,128)S(1)}, f32[16,2,3,1152]{3,1,2,0:T(2,128)}, u32[]{:S(2)}) %copy-start) | copy-done | bytes 442392
  1.0 0.0 copy-start.1
  1.0 1.0 %copy-done.1 = f32[16,2,3,1152]{3,1,2,0:T(2,128)S(1)} copy-done((f32[16,2,3,1152]{3,1,2,0:T(2,128)S(1)}, f32[16,2,3,1152]{3,1,2,0:T(2,128)}, u32[]{:S(2)}) %copy-start.1) | copy-done | bytes 442392
  2.0 0.0 copy-start.2
  2.0 0.9 %copy-done.2 = bf16[144,288]{1,0:T(8,128)(2,1)S(1)} copy-done((bf16[144,288]{1,0:T(8,128)(2,1)S(1)}, bf16[144,288]{1,0:T(8,128)(2,1)}, u32[]{:S(2)}) %copy-start.2) | copy-done | bytes 82968
  2.9 0.0 copy-start.3
  2.9 1.1 %copy-done.3 = bf16[256,1536]{1,0:T(8,128)(2,1)S(1)} copy-done((bf16[256,1536]{1,0:T(8,128)(2,1)S(1)}, bf16[256,1536]{1,0:T(8,128)(2,1)}, u32[]{:S(2)}) %copy-start.3) | copy-done | bytes 786456
  4.1 0.0 copy-start.4
  4.1 1.1 %copy-done.4 = bf16[512,768]{1,0:T(8,128)(2,1)S(1)} copy-done((bf16[512,768]{1,0:T(8,128)(2,1)S(1)}, bf16[512,768]{1,0:T(8,128)(2,1)}, u32[]{:S(2)}) %copy-start.4) | copy-done | bytes 786456
  5.2 44.9 %shard_map.55 = f32[96,1152]{1,0:T(8,128)S(1)} custom-call(f32[16,3,2,1152]{3,2,1,0:T(2,128)S(1)} %bitcast.5, f32[16,3,2,1152]{3,2,1,0:T(2,128)S(1)} %bitcast.6, bf16[144,288]{1,0:T(8,128)(2,1)S(1)} %copy-done.2, bf16[512,768]{1,0:T(8,128)(2,1)S(1)} %copy-done.4, bf16[256,1536]{1,0:T(8,128)(2,1)S(1)} %copy-done.3), custom_call_target="tpu_custom_call" | custom-call | flops 2000000000 | bytes 8000000 | tf_op jit(solution)/shard_map/pallas_call | solution.py:301
  50.1 0.3 reshape.3
  50.4 0.8 %copy.8 = f32[3,16,2,1152]{3,2,0,1:T(2,128)} copy(f32[3,16,2,1152]{3,2,1,0:T(2,128)S(1)} %reshape.3) | data formatting | bytes 884736 | tf_op jit(solution)/shard_map/reshape | solution.py:325
Async XLA Ops:
  0.0 1.0 %copy-start = (f32[16,2,3,1152]{3,1,2,0:T(2,128)S(1)}, f32[16,2,3,1152]{3,1,2,0:T(2,128)}, u32[]{:S(2)}) copy-start(f32[16,2,3,1152]{3,1,2,0:T(2,128)} %param.5) | copy-start | bytes 1327108
  1.0 1.0 %copy-start.1 = (f32[16,2,3,1152]{3,1,2,0:T(2,128)S(1)}, f32[16,2,3,1152]{3,1,2,0:T(2,128)}, u32[]{:S(2)}) copy-start(f32[16,2,3,1152]{3,1,2,0:T(2,128)} %param.6) | copy-start | bytes 1327108
  2.0 0.9 %copy-start.2 = (bf16[144,288]{1,0:T(8,128)(2,1)S(1)}, bf16[144,288]{1,0:T(8,128)(2,1)}, u32[]{:S(2)}) copy-start(bf16[144,288]{1,0:T(8,128)(2,1)} %w_ref.1) | copy-start | bytes 248836
  2.9 1.1 %copy-start.3 = (bf16[256,1536]{1,0:T(8,128)(2,1)S(1)}, bf16[256,1536]{1,0:T(8,128)(2,1)}, u32[]{:S(2)}) copy-start(bf16[256,1536]{1,0:T(8,128)(2,1)} %constant.5.clone.ti_ref) | copy-start | bytes 2359300
  4.1 1.1 %copy-start.4 = (bf16[512,768]{1,0:T(8,128)(2,1)S(1)}, bf16[512,768]{1,0:T(8,128)(2,1)}, u32[]{:S(2)}) copy-start(bf16[512,768]{1,0:T(8,128)(2,1)} %constant.4.clone.tf_ref) | copy-start | bytes 2359300

commit v2 on v1

v2 whole, which is shorter than its diff:
```python
import functools
import math

import jax
import jax.numpy as jnp
import ml_dtypes
import numpy as np
from jax import lax
from jax.experimental import pallas as pl
from jax.experimental.pallas import tpu as pltpu
from jax.sharding import PartitionSpec as P

LANES = 128
REST = 32
MESH = pl.DeviceIdType.MESH


def product(left, right):
    return jnp.dot(left, right, precision=lax.Precision.HIGHEST, preferred_element_type=jnp.float32)


def per_device(lesser, greater_transposed, coulomb):
    lesser_all, greater_all = (
        lax.all_to_all(lesser, "energy", split_axis=3, concat_axis=0, tiled=True),
        lax.all_to_all(greater_transposed, "energy", split_axis=3, concat_axis=0, tiled=True),
    )
    energies = lesser_all.shape[0]
    columns_here = lesser_all.shape[2]
    rows_here = lesser_all.shape[3]
    padded = 2 * energies
    lesser_re = lesser_all[:, 0].reshape(energies, -1)
    lesser_im = lesser_all[:, 1].reshape(energies, -1)
    greater_re = greater_all[:, 0].reshape(energies, -1)
    greater_im = greater_all[:, 1].reshape(energies, -1)
    frequency = lax.broadcasted_iota(jnp.int32, (padded, energies), 0)
    position = lax.broadcasted_iota(jnp.int32, (padded, energies), 1)
    phases = frequency * position % padded
    angles = phases.astype(jnp.float32) * (2.0 * math.pi / padded)
    cos_table = jnp.cos(angles)
    sin_table = jnp.sin(angles)
    left_re = product(cos_table, lesser_re) + product(sin_table, lesser_im)
    left_im = product(cos_table, lesser_im) - product(sin_table, lesser_re)
    right_re = product(cos_table, greater_re) - product(sin_table, greater_im)
    right_im = product(cos_table, greater_im) + product(sin_table, greater_re)
    mixed_re = left_re * right_re - left_im * right_im
    mixed_im = left_re * right_im + left_im * right_re
    corr_re = (product(cos_table.T, mixed_re) - product(sin_table.T, mixed_im)) / padded
    corr_im = (product(cos_table.T, mixed_im) + product(sin_table.T, mixed_re)) / padded
    factor = 1.0 / math.sqrt(energies)
    polar_re = (corr_im * factor).reshape(energies, columns_here, rows_here)
    polar_im = (-corr_re * factor).reshape(energies, columns_here, rows_here)
    polarized = jnp.stack([polar_re, polar_im], axis=1).astype(jnp.bfloat16)
    coulomb_wide = lax.all_gather(coulomb, "col", axis=1, tiled=True)
    order = coulomb_wide.shape[1]
    returned = lax.all_to_all(polarized, "energy", split_axis=0, concat_axis=3, tiled=True)
    flattened = returned.reshape(-1, order)
    running = jnp.dot(
        flattened,
        lax.all_gather(coulomb_wide, "energy", axis=0, tiled=True),
        preferred_element_type=jnp.float32,
    )
    screened = running.reshape(returned.shape)
    return screened


def split_table(table):
    high = table.astype(ml_dtypes.bfloat16)
    low = (table - high.astype(np.float64)).astype(ml_dtypes.bfloat16)
    return np.concatenate([high, high, low], axis=1)


def tables(energies):
    padded = 2 * energies
    angle = 2.0 * math.pi / padded * (np.outer(np.arange(padded), np.arange(energies)) % padded)
    cos, sin = np.cos(angle), np.sin(angle)
    forward_re = np.stack([cos, sin], axis=2).reshape(padded, padded)
    forward_im = np.stack([-sin, cos], axis=2).reshape(padded, padded)
    forward = np.concatenate([forward_re, forward_im], axis=0)
    scale = 1.0 / (padded * math.sqrt(energies))
    corr_re = np.concatenate([cos.T, -sin.T], axis=1)
    corr_im = np.concatenate([sin.T, cos.T], axis=1)
    inverse = np.stack([corr_im, -corr_re], axis=1).reshape(padded, 2 * padded) * scale
    return split_table(forward), split_table(inverse)


def high_low(x):
    high = x.astype(jnp.bfloat16)
    return high, (x - high.astype(jnp.float32)).astype(jnp.bfloat16)


def kernel(n, m, l_hbm, r_hbm, w_hbm, tf_hbm, ti_hbm, o_ref, l_ref, r_ref, w_ref, tf_ref, ti_ref,
           give, take, polar, panel, coul, lr_send, lr_recv, p_send, p_recv, c_send, c_recv, own_sem, load_sem):
    here_e, here_c = lax.axis_index("energy"), lax.axis_index("col")
    block, cols, _, order = l_ref.shape
    tiles_k = order // LANES
    total = cols * tiles_k
    full, extra = total // n, total % n
    slots = full + (1 if extra else 0)
    rows = 2 * block
    depth, width = w_ref.shape
    wide = width - REST
    third = depth // 3
    groups = [(start, min(start + 2, slots)) for start in range(0, slots, 2)]

    loads = [pltpu.make_async_copy(a, b, load_sem.at[i]) for i, (a, b) in enumerate(
        [(l_hbm, l_ref), (r_hbm, r_ref), (w_hbm, w_ref), (tf_hbm, tf_ref), (ti_hbm, ti_ref)])]
    for load in loads:
        load.start()

    z, y = here_e // 2, lax.rem(here_e, 2)
    x, core = here_c // 2, lax.rem(here_c, 2)
    nz = n // 2
    peer_y = z * 2 + 1 - y
    peer_x = (1 - x) * 2 + core
    peer_core = x * 2 + 1 - core

    barrier = pltpu.get_barrier_semaphore()
    for s in range(1, n):
        pl.semaphore_signal(barrier, inc=1, device_id={"energy": lax.rem(here_e + s, n)}, device_id_type=MESH)
    for peer in (peer_x, peer_core):
        pl.semaphore_signal(barrier, inc=1, device_id={"col": peer}, device_id_type=MESH)

    sign = jnp.where(lax.broadcasted_iota(jnp.int32, (rows, LANES), 0) % 2 == 0, 1.0, -1.0)

    def pack(t):
        j, d = t // n, t % n
        c, k = t // tiles_k, t % tiles_k
        lanes = slice(k * LANES, (k + 1) * LANES)
        high, low = high_low(l_ref[:, c, :, lanes].reshape(rows, LANES))
        give[d, j, 0:rows] = high
        give[d, j, rows:2 * rows] = low
        right = r_ref[:, c, :, lanes].reshape(rows, LANES) * sign
        give[d, j, 2 * rows:3 * rows] = right.astype(jnp.bfloat16)

    def exchange(source, target, send_sems, recv_sems, send_if, recv_if):
        out = []
        for i, (start, stop) in enumerate(groups):
            copies = []
            for s in range(1, n):
                dev = lax.rem(here_e + s, n)
                whole = min(stop, full) - start
                if whole:
                    copies.append((pltpu.make_async_remote_copy(
                        src_ref=source(start, whole, dev), dst_ref=target(start, whole),
                        send_sem=send_sems.at[2 * i, s], recv_sem=recv_sems.at[2 * i, s],
                        device_id={"energy": dev}, device_id_type=MESH), None, None))
                if stop > full:
                    copies.append((pltpu.make_async_remote_copy(
                        src_ref=source(full, 1, dev), dst_ref=target(full, 1),
                        send_sem=send_sems.at[2 * i + 1, s], recv_sem=recv_sems.at[2 * i + 1, s],
                        device_id={"energy": dev}, device_id_type=MESH), send_if(s), recv_if(s)))
            out.append(copies)
        return out

    def when(cond, f):
        if cond is None:
            f()
        else:
            pl.when(cond)(f)

    panels = exchange(
        lambda a, w, dev: give.at[dev, pl.ds(a, w)], lambda a, w: take.at[pl.ds(a, w), here_e],
        lr_send, lr_recv, lambda s: lax.rem(here_e + s, n) < extra, lambda s: here_e < extra)
    back = exchange(
        lambda a, w, dev: polar.at[pl.ds(a, w), dev], lambda a, w: panel.at[pl.ds(a, w), here_e],
        p_send, p_recv, lambda s: here_e < extra, lambda s: lax.rem(here_e + n - s, n) < extra)

    places = [(0, 0)] + [(way, s) for s in range(1, nz) for way in (1, -1)]

    def share(index, e, c, dev):
        return pltpu.make_async_remote_copy(
            src_ref=coul.at[e, c], dst_ref=coul.at[e, c], send_sem=c_send.at[index],
            recv_sem=c_recv.at[index], device_id=dev, device_id_type=MESH)

    def inside(position):
        return (position >= 0) & (position < nz)

    count = len(places)
    iz, iy, ix, ic = 0, count, 2 * count, 4 * count
    held, line, line_if, over_y, over_x, over_core = {}, {}, {}, {}, {}, {}
    for k, (way, s) in enumerate(places):
        zk = lax.rem(z - way * s + nz, nz)
        held[k] = None if k == 0 else inside(z - way * s)
        owner = (zk * 2 + y, zk * 2 + 1 - y)
        over_y[k] = share(iy + k, owner[0], here_c, {"energy": peer_y})
        for b in range(2):
            over_x[k, b] = share(ix + 2 * k + b, owner[b], here_c, {"col": peer_x})
            for a in range(2):
                over_core[k, b, a] = share(
                    ic + 4 * k + 2 * b + a, owner[b], here_c if a == 0 else peer_x, {"col": peer_core})
        if k:
            before = lax.rem(z - way * (s - 1) + nz, nz)
            line[k] = share(iz + k, before * 2 + y, here_c, {"energy": lax.rem(z + way + nz, nz) * 2 + y})
            line_if[k] = inside(z - way * (s - 1)) & inside(z + way)

    loads[0].wait()
    loads[1].wait()
    first = groups[0][1] * n
    for t in range(min(first, total)):
        pack(t)
    pl.semaphore_wait(barrier, n - 1 + 2)
    for cp, cond, _ in panels[0]:
        when(cond, cp.start)

    loads[2].wait()
    w = w_ref[...]
    coul[here_e, here_c, 0:depth] = w[:, 0:LANES]
    coul[here_e, here_c, depth:2 * depth] = w[:, LANES:2 * LANES]
    rest = w[:, wide:].astype(jnp.float32)
    packed = jnp.concatenate(
        [rest[q * third:(q + 1) * third] for q in range(3)] + [jnp.zeros((third, LANES - 3 * REST), jnp.float32)],
        axis=1)
    coul[here_e, here_c, 2 * depth:2 * depth + third] = packed.astype(jnp.bfloat16)
    for k, (way, s) in enumerate(places):
        if s == 1:
            when(line_if[k], line[k].start)
    over_y[0].start()
    over_x[0, 0].start()
    over_core[0, 0, 0].start()

    for t in range(first, total):
        pack(t)
    for copies in panels[1:]:
        for cp, cond, _ in copies:
            when(cond, cp.start)
    own = pltpu.make_async_copy(give.at[here_e], take.at[:, here_e], own_sem.at[0])
    own.start()

    def relay():
        for k, (way, s) in enumerate(places):
            if k == 0:
                continue

            def pass_on(k=k, s=s, way=way):
                line[k].wait_recv()
                if s + 1 < nz:
                    after = places.index((way, s + 1))
                    pl.when(line_if[after])(line[after].start)
                over_y[k].start()
                over_x[k, 0].start()
                over_core[k, 0, 0].start()

            when(held[k], pass_on)
        for k in range(count):

            def pass_y(k=k):
                over_y[k].wait_recv()
                over_x[k, 1].start()
                over_core[k, 1, 0].start()

            when(held[k], pass_y)

    span = n * rows

    def correlate(i):
        start, stop = groups[i]
        for cp, _, cond in panels[i]:
            when(cond, cp.wait_recv)

        def piece(p):
            return jnp.concatenate(
                [take[j, :, p * rows:(p + 1) * rows].reshape(span, LANES) for j in range(start, stop)], axis=1)

        l_high, l_low, r_high = piece(0), piece(1), piece(2)
        left = jnp.dot(tf_ref[...], jnp.concatenate([l_high, l_low, l_high], axis=0),
                       preferred_element_type=jnp.float32)
        right = jnp.dot(tf_ref[:, span:], jnp.concatenate([r_high, r_high], axis=0),
                        preferred_element_type=jnp.float32)
        a, b = left[:span], left[span:]
        c, d = right[:span], right[span:]
        mixed = jnp.concatenate([a * c + b * d, b * c - a * d], axis=0)
        m_high, m_low = high_low(mixed)
        polarized = jnp.dot(ti_ref[...], jnp.concatenate([m_high, m_low, m_high], axis=0),
                            preferred_element_type=jnp.float32).astype(jnp.bfloat16)
        for j in range(start, stop):
            polar[j] = polarized[:, (j - start) * LANES:(j - start + 1) * LANES].reshape(n, rows, LANES)
        for cp, cond, _ in back[i]:
            when(cond, cp.start)

    loads[3].wait()
    loads[4].wait()
    own.wait()
    for i in range(len(groups)):
        correlate(i)
        if i == 0:
            relay()
    own_p = pltpu.make_async_copy(polar.at[:, here_e], panel.at[:, here_e], own_sem.at[1])
    own_p.start()

    for k in range(count):

        def pass_x(k=k):
            for b in range(2):
                over_x[k, b].wait_recv()
                over_core[k, b, 1].start()

        when(held[k], pass_x)
    for k in range(count):

        def arrive(k=k):
            for b in range(2):
                for a in range(2):
                    over_core[k, b, a].wait_recv()

        when(held[k], arrive)

    lane = lax.broadcasted_iota(jnp.int32, (third, LANES), 1)
    rests = []
    for g in range(n):
        for q in range(3):
            acc = jnp.zeros((third, LANES), jnp.float32)
            for cc in range(m):
                u = coul[g, cc, 2 * depth:2 * depth + third].astype(jnp.float32)
                shift = (cc - q) * REST % LANES
                if shift:
                    u = pltpu.roll(u, shift, 1)
                acc = jnp.where((lane >= cc * REST) & (lane < (cc + 1) * REST), u, acc)
            rests.append(acc.astype(jnp.bfloat16))
    rest_all = jnp.concatenate(rests, axis=0)

    own_p.wait()
    for copies in back:
        for cp, _, cond in copies:
            when(cond, cp.wait_recv)

    flat = jnp.concatenate(
        [jnp.concatenate([panel[t // n, t % n] for t in range(c * tiles_k, (c + 1) * tiles_k)], axis=1)
         for c in range(cols)], axis=0)
    rest_out = jnp.dot(flat, rest_all, preferred_element_type=jnp.float32)
    pieces = []
    for cc in range(m):
        weight = jnp.concatenate(
            [coul[:, cc, h * depth:(h + 1) * depth].reshape(n * depth, LANES) for h in range(2)], axis=1)
        pieces.append(jnp.dot(flat, weight, preferred_element_type=jnp.float32))
        pieces.append(rest_out[:, cc * REST:(cc + 1) * REST])
    o_ref[...] = jnp.concatenate(pieces, axis=1)

    for copies in panels + back:
        for cp, cond, _ in copies:
            when(cond, cp.wait_send)
    for k in range(count):

        def sent(k=k):
            over_y[k].wait_send()
            for b in range(2):
                over_x[k, b].wait_send()
                for a in range(2):
                    over_core[k, b, a].wait_send()

        when(held[k], sent)
        if k:
            when(line_if[k], line[k].wait_send)


def fused(n, m, lesser, greater_transposed, coulomb):
    block, _, cols, order = lesser.shape
    depth, width = coulomb.shape
    energies = n * block
    total = cols * order // LANES
    slots = -(-total // n)
    rows = 2 * block
    forward, inverse = tables(energies)
    passes = 2 * (-(-slots // 2))
    places = 1 + 2 * (n // 2 - 1)
    out = pl.pallas_call(
        functools.partial(kernel, n, m),
        out_shape=jax.ShapeDtypeStruct((cols * rows, order), jnp.float32),
        in_specs=[pl.BlockSpec(memory_space=pl.ANY)] * 5,
        out_specs=pl.BlockSpec(memory_space=pltpu.VMEM),
        scratch_shapes=[
            pltpu.VMEM((block, cols, 2, order), jnp.float32),
            pltpu.VMEM((block, cols, 2, order), jnp.float32),
            pltpu.VMEM((depth, width), jnp.bfloat16),
            pltpu.VMEM(forward.shape, jnp.bfloat16),
            pltpu.VMEM(inverse.shape, jnp.bfloat16),
            pltpu.VMEM((n, slots, 3 * rows, LANES), jnp.bfloat16),
            pltpu.VMEM((slots, n, 3 * rows, LANES), jnp.bfloat16),
            pltpu.VMEM((slots, n, rows, LANES), jnp.bfloat16),
            pltpu.VMEM((slots, n, rows, LANES), jnp.bfloat16),
            pltpu.VMEM((n, m, 2 * depth + depth // 3, LANES), jnp.bfloat16),
            pltpu.SemaphoreType.DMA((passes, n)),
            pltpu.SemaphoreType.DMA((passes, n)),
            pltpu.SemaphoreType.DMA((passes, n)),
            pltpu.SemaphoreType.DMA((passes, n)),
            pltpu.SemaphoreType.DMA((8 * places,)),
            pltpu.SemaphoreType.DMA((8 * places,)),
            pltpu.SemaphoreType.DMA((2,)),
            pltpu.SemaphoreType.DMA((5,)),
        ],
        compiler_params=pltpu.CompilerParams(
            collective_id=0, has_side_effects=True, vmem_limit_bytes=63 * 2**20),
        cost_estimate=pl.CostEstimate(flops=2_000_000_000, bytes_accessed=8_000_000, transcendentals=0),
    )(lesser.transpose(0, 2, 1, 3), greater_transposed.transpose(0, 2, 1, 3), coulomb,
      jnp.asarray(forward), jnp.asarray(inverse))
    return out.reshape(cols, block, 2, order).transpose(1, 2, 0, 3)


def solution(mesh):
    placed = (P("energy", None, "col", None), P("energy", None, "col", None), P("energy", "col"))
    n, m = mesh.shape["energy"], mesh.shape["col"]

    def local(lesser, greater_transposed, coulomb):
        depth, width = coulomb.shape
        fits = (m == 4 and n % 2 == 0 and depth % 48 == 0 and width == 2 * LANES + REST
                and lesser.shape[0] % 8 == 0 and lesser.shape[3] % LANES == 0)
        if fits:
            return fused(n, m, lesser, greater_transposed, coulomb)
        return per_device(lesser, greater_transposed, coulomb)

    return jax.shard_map(
        local,
        mesh=mesh,
        in_specs=placed,
        out_specs=P("energy", None, "col", None),
        check_vma=False,
    )
```

time: 51.5 us -> 50.8 us (0.986)
  local copies, waits for them, and re-layouts: 6.25 us -> 2.07 us
  Pallas kernels: 44.9 us -> 48.6 us
    unnamed x10 -> x0, local copies, waits for them, and re-layouts: 5.19 us -> none
    pallas_call x1, Pallas kernels: 44.9 us -> 48.6 us  [fused(): pl.pallas_call(functools.partial(kernel, n, m), out_shape=jax.ShapeDtypeS...]
    reshape x2, local copies, waits for them, and re-layouts: 1.06 us -> 2.07 us  [fused(): return out.reshape(cols, block, 2, order).transpose(1, 2, 0, 3)]
where the time goes in v2:
time: 50.8 us; the launch traced here: 50.7 us
  Pallas kernels  48.6 us (96%)
  local copies, waits for them, and re-layouts  2.07 us (4%)
    pallas_call x1, Pallas kernels, fused(): pl.pallas_call(functools.partial(kernel, n, m), out_shape=jax.ShapeDtypeS...  48.6 us
    reshape x2, local copies, waits for them, and re-layouts, fused(): return out.reshape(cols, block, 2, order).transpose(1, 2, 0, 3)  2.07 us

profile of v2, /device:TPU:1, one launch (start us, length us, event | category | flops | bytes accessed | tf_op | source)
XLA Modules:
  0.0 50.7 jit_solution(166005740613998513)
XLA Ops:
  0.0 48.6 %shard_map.55 = f32[96,1152]{1,0:T(8,128)} custom-call(f32[16,3,2,1152]{3,2,1,0:T(2,128)} %bitcast.5, f32[16,3,2,1152]{3,2,1,0:T(2,128)} %bitcast.6, bf16[144,288]{1,0:T(8,128)(2,1)} %w_hbm.1, bf16[512,768]{1,0:T(8,128)(2,1)} %constant.4.clone.tf_hbm, bf16[256,1536]{1,0:T(8,128)(2,1)} %constant.5.clone.ti_hbm), custom_call_target="tpu_custom_call" | custom-call | flops 2000000000 | bytes 8000000 | tf_op jit(solution)/shard_map/pallas_call | solution.py:365
  48.6 1.3 %reshape.3 = f32[3,16,2,1152]{3,2,1,0:T(2,128)S(1)} reshape(f32[96,1152]{1,0:T(8,128)} %shard_map.55) | data formatting | bytes 884736 | tf_op jit(solution)/shard_map/reshape | solution.py:395
  49.8 0.8 %copy.8 = f32[3,16,2,1152]{3,2,0,1:T(2,128)} copy(f32[3,16,2,1152]{3,2,1,0:T(2,128)S(1)} %reshape.3) | data formatting | bytes 884736 | tf_op jit(solution)/shard_map/reshape | solution.py:395

commit v3 on v2

--- a/solution.py
+++ b/solution.py
@@ -104,8 +104,8 @@
 
     loads = [pltpu.make_async_copy(a, b, load_sem.at[i]) for i, (a, b) in enumerate(
         [(l_hbm, l_ref), (r_hbm, r_ref), (w_hbm, w_ref), (tf_hbm, tf_ref), (ti_hbm, ti_ref)])]
-    for load in loads:
-        load.start()
+    for i in (2, 0, 1, 3, 4):
+        loads[i].start()
 
     z, y = here_e // 2, lax.rem(here_e, 2)
     x, core = here_c // 2, lax.rem(here_c, 2)
@@ -193,15 +193,6 @@
             line[k] = share(iz + k, before * 2 + y, here_c, {"energy": lax.rem(z + way + nz, nz) * 2 + y})
             line_if[k] = inside(z - way * (s - 1)) & inside(z + way)
 
-    loads[0].wait()
-    loads[1].wait()
-    first = groups[0][1] * n
-    for t in range(min(first, total)):
-        pack(t)
-    pl.semaphore_wait(barrier, n - 1 + 2)
-    for cp, cond, _ in panels[0]:
-        when(cond, cp.start)
-
     loads[2].wait()
     w = w_ref[...]
     coul[here_e, here_c, 0:depth] = w[:, 0:LANES]
@@ -211,12 +202,21 @@
         [rest[q * third:(q + 1) * third] for q in range(3)] + [jnp.zeros((third, LANES - 3 * REST), jnp.float32)],
         axis=1)
     coul[here_e, here_c, 2 * depth:2 * depth + third] = packed.astype(jnp.bfloat16)
+    pl.semaphore_wait(barrier, n - 1 + 2)
     for k, (way, s) in enumerate(places):
         if s == 1:
             when(line_if[k], line[k].start)
     over_y[0].start()
     over_x[0, 0].start()
     over_core[0, 0, 0].start()
+
+    loads[0].wait()
+    loads[1].wait()
+    first = groups[0][1] * n
+    for t in range(min(first, total)):
+        pack(t)
+    for cp, cond, _ in panels[0]:
+        when(cond, cp.start)
 
     for t in range(first, total):
         pack(t)
@@ -226,9 +226,9 @@
     own = pltpu.make_async_copy(give.at[here_e], take.at[:, here_e], own_sem.at[0])
     own.start()
 
-    def relay():
+    def relay_z(distance):
         for k, (way, s) in enumerate(places):
-            if k == 0:
+            if s != distance:
                 continue
 
             def pass_on(k=k, s=s, way=way):
@@ -241,7 +241,11 @@
                 over_core[k, 0, 0].start()
 
             when(held[k], pass_on)
-        for k in range(count):
+
+    def relay_y(distance):
+        for k, (way, s) in enumerate(places):
+            if s != distance:
+                continue
 
             def pass_y(k=k):
                 over_y[k].wait_recv()
@@ -277,13 +281,21 @@
         for cp, cond, _ in back[i]:
             when(cond, cp.start)
 
+    relay_z(1)
+    relay_y(0)
+    for s in range(2, nz - 1):
+        relay_z(s)
+        relay_y(s - 1)
     loads[3].wait()
     loads[4].wait()
     own.wait()
-    for i in range(len(groups)):
+    correlate(0)
+    if nz > 2:
+        relay_z(nz - 1)
+        relay_y(nz - 2)
+    relay_y(nz - 1)
+    for i in range(1, len(groups)):
         correlate(i)
-        if i == 0:
-            relay()
     own_p = pltpu.make_async_copy(polar.at[:, here_e], panel.at[:, here_e], own_sem.at[1])
     own_p.start()
 
@@ -333,7 +345,9 @@
             [coul[:, cc, h * depth:(h + 1) * depth].reshape(n * depth, LANES) for h in range(2)], axis=1)
         pieces.append(jnp.dot(flat, weight, preferred_element_type=jnp.float32))
         pieces.append(rest_out[:, cc * REST:(cc + 1) * REST])
-    o_ref[...] = jnp.concatenate(pieces, axis=1)
+    screened = jnp.concatenate(pieces, axis=1)
+    for c in range(cols):
+        o_ref[:, c] = screened[c * rows:(c + 1) * rows].reshape(block, 2, order)
 
     for copies in panels + back:
         for cp, cond, _ in copies:
@@ -364,7 +378,7 @@
     places = 1 + 2 * (n // 2 - 1)
     out = pl.pallas_call(
         functools.partial(kernel, n, m),
-        out_shape=jax.ShapeDtypeStruct((cols * rows, order), jnp.float32),
+        out_shape=jax.ShapeDtypeStruct((block, cols, 2, order), jnp.float32),
         in_specs=[pl.BlockSpec(memory_space=pl.ANY)] * 5,
         out_specs=pl.BlockSpec(memory_space=pltpu.VMEM),
         scratch_shapes=[
@@ -392,7 +406,7 @@
         cost_estimate=pl.CostEstimate(flops=2_000_000_000, bytes_accessed=8_000_000, transcendentals=0),
     )(lesser.transpose(0, 2, 1, 3), greater_transposed.transpose(0, 2, 1, 3), coulomb,
       jnp.asarray(forward), jnp.asarray(inverse))
-    return out.reshape(cols, block, 2, order).transpose(1, 2, 0, 3)
+    return out.transpose(0, 2, 1, 3)
 
 
 def solution(mesh):

time: 50.8 us -> 45.9 us (0.904)
  Pallas kernels: 48.6 us -> 43.7 us
    pallas_call x1, Pallas kernels: 48.6 us -> 43.7 us  [fused(): pl.pallas_call(functools.partial(kernel, n, m), out_shape=jax.ShapeDtypeS...]
    reshape x2 -> x0, local copies, waits for them, and re-layouts: 2.07 us -> none  [fused(): return out.reshape(cols, block, 2, order).transpose(1, 2, 0, 3)]
    unnamed x0 -> x1, local copies, waits for them, and re-layouts: none -> 1.82 us
where the time goes in v3:
time: 45.9 us; the launch traced here: 45.5 us
  Pallas kernels  43.7 us (95%)
  local copies, waits for them, and re-layouts  1.82 us (4%)
    pallas_call x1, Pallas kernels, fused(): pl.pallas_call(functools.partial(kernel, n, m), out_shape=jax.ShapeDtypeS...  43.7 us
    unnamed x1, local copies, waits for them, and re-layouts  1.82 us

profile of v3, /device:TPU:1, one launch (start us, length us, event | category | flops | bytes accessed | tf_op | source)
XLA Modules:
  0.0 45.5 jit_solution(13176438481880425860)
XLA Ops:
  0.0 43.7 %shard_map.55 = f32[16,3,2,1152]{3,2,1,0:T(2,128)} custom-call(f32[16,3,2,1152]{3,2,1,0:T(2,128)} %bitcast.4, f32[16,3,2,1152]{3,2,1,0:T(2,128)} %bitcast.5, bf16[144,288]{1,0:T(8,128)(2,1)} %w_hbm.1, bf16[512,768]{1,0:T(8,128)(2,1)} %constant.4.clone.tf_hbm, bf16[256,1536]{1,0:T(8,128)(2,1)} %constant.5.clone.ti_hbm), custom_call_target="tpu_custom_call" | custom-call | flops 2000000000 | bytes 8000000 | tf_op jit(solution)/shard_map/pallas_call | solution.py:379
  43.7 1.8 %copy.7 = f32[16,2,3,1152]{3,1,2,0:T(2,128)} copy(f32[16,2,3,1152]{3,1,2,0:T(2,128)} %bitcast.3) | data formatting | bytes 884736

commit v4 on v3

--- a/solution.py
+++ b/solution.py
@@ -100,7 +100,12 @@
     depth, width = w_ref.shape
     wide = width - REST
     third = depth // 3
-    groups = [(start, min(start + 2, slots)) for start in range(0, slots, 2)]
+    lead = 1 if extra else 0
+    groups = [(0, slots - 1), (slots - 1, slots)] if slots > 1 else [(0, 1)]
+
+    def slot(t):
+        return (0, t) if t < extra else ((t - extra) // n + lead, (t - extra) % n)
+
 
     loads = [pltpu.make_async_copy(a, b, load_sem.at[i]) for i, (a, b) in enumerate(
         [(l_hbm, l_ref), (r_hbm, r_ref), (w_hbm, w_ref), (tf_hbm, tf_ref), (ti_hbm, ti_ref)])]
@@ -123,8 +128,8 @@
     sign = jnp.where(lax.broadcasted_iota(jnp.int32, (rows, LANES), 0) % 2 == 0, 1.0, -1.0)
 
     def pack(t):
-        j, d = t // n, t % n
-        c, k = t // tiles_k, t % tiles_k
+        j, d = slot(t)
+        c, k = t % cols, t // cols
         lanes = slice(k * LANES, (k + 1) * LANES)
         high, low = high_low(l_ref[:, c, :, lanes].reshape(rows, LANES))
         give[d, j, 0:rows] = high
@@ -138,15 +143,15 @@
             copies = []
             for s in range(1, n):
                 dev = lax.rem(here_e + s, n)
-                whole = min(stop, full) - start
-                if whole:
+                begin = max(start, lead)
+                if stop > begin:
                     copies.append((pltpu.make_async_remote_copy(
-                        src_ref=source(start, whole, dev), dst_ref=target(start, whole),
+                        src_ref=source(begin, stop - begin, dev), dst_ref=target(begin, stop - begin),
                         send_sem=send_sems.at[2 * i, s], recv_sem=recv_sems.at[2 * i, s],
                         device_id={"energy": dev}, device_id_type=MESH), None, None))
-                if stop > full:
+                if start < lead:
                     copies.append((pltpu.make_async_remote_copy(
-                        src_ref=source(full, 1, dev), dst_ref=target(full, 1),
+                        src_ref=source(0, 1, dev), dst_ref=target(0, 1),
                         send_sem=send_sems.at[2 * i + 1, s], recv_sem=recv_sems.at[2 * i + 1, s],
                         device_id={"energy": dev}, device_id_type=MESH), send_if(s), recv_if(s)))
             out.append(copies)
@@ -212,8 +217,8 @@
 
     loads[0].wait()
     loads[1].wait()
-    first = groups[0][1] * n
-    for t in range(min(first, total)):
+    first = extra + (groups[0][1] - lead) * n
+    for t in range(first):
         pack(t)
     for cp, cond, _ in panels[0]:
         when(cond, cp.start)
@@ -330,21 +335,33 @@
             rests.append(acc.astype(jnp.bfloat16))
     rest_all = jnp.concatenate(rests, axis=0)
 
+    def multiply(low, high):
+        flat = jnp.concatenate(
+            [jnp.concatenate([panel[slot(k * cols + c)] for k in range(low, high)], axis=1) for c in range(cols)],
+            axis=0)
+        part = slice(low * LANES, high * LANES)
+        out = []
+        for cc in range(m):
+            weight = jnp.concatenate(
+                [coul[:, cc, h * depth:(h + 1) * depth].reshape(n * depth, LANES)[part] for h in range(2)], axis=1)
+            out.append(jnp.dot(flat, weight, preferred_element_type=jnp.float32))
+        out.append(jnp.dot(flat, rest_all[part], preferred_element_type=jnp.float32))
+        return out
+
     own_p.wait()
-    for copies in back:
+    cut = first // cols
+    sums = None
+    for i, copies in enumerate(back):
         for cp, _, cond in copies:
             when(cond, cp.wait_recv)
-
-    flat = jnp.concatenate(
-        [jnp.concatenate([panel[t // n, t % n] for t in range(c * tiles_k, (c + 1) * tiles_k)], axis=1)
-         for c in range(cols)], axis=0)
-    rest_out = jnp.dot(flat, rest_all, preferred_element_type=jnp.float32)
+        low, high = (0 if i == 0 else cut), (tiles_k if i == len(back) - 1 else cut)
+        if high > low:
+            terms = multiply(low, high)
+            sums = terms if sums is None else [p + q for p, q in zip(sums, terms)]
     pieces = []
     for cc in range(m):
-        weight = jnp.concatenate(
-            [coul[:, cc, h * depth:(h + 1) * depth].reshape(n * depth, LANES) for h in range(2)], axis=1)
-        pieces.append(jnp.dot(flat, weight, preferred_element_type=jnp.float32))
-        pieces.append(rest_out[:, cc * REST:(cc + 1) * REST])
+        pieces.append(sums[cc])
+        pieces.append(sums[m][:, cc * REST:(cc + 1) * REST])
     screened = jnp.concatenate(pieces, axis=1)
     for c in range(cols):
         o_ref[:, c] = screened[c * rows:(c + 1) * rows].reshape(block, 2, order)
@@ -374,7 +391,7 @@
     slots = -(-total // n)
     rows = 2 * block
     forward, inverse = tables(energies)
-    passes = 2 * (-(-slots // 2))
+    passes = 4
     places = 1 + 2 * (n // 2 - 1)
     out = pl.pallas_call(
         functools.partial(kernel, n, m),

time: 45.9 us -> 46 us (level)
  no operation moved by 1% of the time
where the time goes in v4:
time: 46 us; the launch traced here: 45.8 us
  Pallas kernels  44 us (96%)
  local copies, waits for them, and re-layouts  1.82 us (4%)
    pallas_call x1, Pallas kernels, fused(): pl.pallas_call(functools.partial(kernel, n, m), out_shape=jax.ShapeDtypeS...  44 us
    unnamed x1, local copies, waits for them, and re-layouts  1.82 us

profile of v4, /device:TPU:1, one launch (start us, length us, event | category | flops | bytes accessed | tf_op | source)
XLA Modules:
  0.0 45.8 jit_solution(683509413209818775)
XLA Ops:
  0.0 44.0 %shard_map.55 = f32[16,3,2,1152]{3,2,1,0:T(2,128)} custom-call(f32[16,3,2,1152]{3,2,1,0:T(2,128)} %bitcast.4, f32[16,3,2,1152]{3,2,1,0:T(2,128)} %bitcast.5, bf16[144,288]{1,0:T(8,128)(2,1)} %w_hbm.1, bf16[512,768]{1,0:T(8,128)(2,1)} %constant.4.clone.tf_hbm, bf16[256,1536]{1,0:T(8,128)(2,1)} %constant.5.clone.ti_hbm), custom_call_target="tpu_custom_call" | custom-call | flops 2000000000 | bytes 8000000 | tf_op jit(solution)/shard_map/pallas_call | solution.py:396
  44.0 1.8 %copy.7 = f32[16,2,3,1152]{3,1,2,0:T(2,128)} copy(f32[16,2,3,1152]{3,1,2,0:T(2,128)} %bitcast.3) | data formatting | bytes 884736

commit v5 on v4

--- a/solution.py
+++ b/solution.py
@@ -259,6 +259,18 @@
 
             when(held[k], pass_y)
 
+    def relay_x(distance):
+        for k, (way, s) in enumerate(places):
+            if s != distance:
+                continue
+
+            def pass_x(k=k):
+                for b in range(2):
+                    over_x[k, b].wait_recv()
+                    over_core[k, b, 1].start()
+
+            when(held[k], pass_x)
+
     span = n * rows
 
     def correlate(i):
@@ -299,19 +311,15 @@
         relay_z(nz - 1)
         relay_y(nz - 2)
     relay_y(nz - 1)
+    for s in range(min(2, nz)):
+        relay_x(s)
     for i in range(1, len(groups)):
         correlate(i)
     own_p = pltpu.make_async_copy(polar.at[:, here_e], panel.at[:, here_e], own_sem.at[1])
     own_p.start()
 
-    for k in range(count):
-
-        def pass_x(k=k):
-            for b in range(2):
-                over_x[k, b].wait_recv()
-                over_core[k, b, 1].start()
-
-        when(held[k], pass_x)
+    for s in range(2, nz):
+        relay_x(s)
     for k in range(count):
 
         def arrive(k=k):

time: 46 us -> 46.1 us (level)
  no operation moved by 1% of the time
where the time goes in v5:
time: 46.1 us; the launch traced here: 45.9 us
  Pallas kernels  44.1 us (96%)
  local copies, waits for them, and re-layouts  1.82 us (4%)
    pallas_call x1, Pallas kernels, fused(): pl.pallas_call(functools.partial(kernel, n, m), out_shape=jax.ShapeDtypeS...  44.1 us
    unnamed x1, local copies, waits for them, and re-layouts  1.82 us

profile of v5, /device:TPU:1, one launch (start us, length us, event | category | flops | bytes accessed | tf_op | source)
XLA Modules:
  0.0 45.9 jit_solution(6504006425520335806)
XLA Ops:
  0.0 44.1 %shard_map.55 = f32[16,3,2,1152]{3,2,1,0:T(2,128)} custom-call(f32[16,3,2,1152]{3,2,1,0:T(2,128)} %bitcast.4, f32[16,3,2,1152]{3,2,1,0:T(2,128)} %bitcast.5, bf16[144,288]{1,0:T(8,128)(2,1)} %w_hbm.1, bf16[512,768]{1,0:T(8,128)(2,1)} %constant.4.clone.tf_hbm, bf16[256,1536]{1,0:T(8,128)(2,1)} %constant.5.clone.ti_hbm), custom_call_target="tpu_custom_call" | custom-call | flops 2000000000 | bytes 8000000 | tf_op jit(solution)/shard_map/pallas_call | solution.py:404
  44.1 1.8 %copy.7 = f32[16,2,3,1152]{3,1,2,0:T(2,128)} copy(f32[16,2,3,1152]{3,1,2,0:T(2,128)} %bitcast.3) | data formatting | bytes 884736

commit v6 on v5

--- a/solution.py
+++ b/solution.py
@@ -303,14 +303,14 @@
     for s in range(2, nz - 1):
         relay_z(s)
         relay_y(s - 1)
+    if nz > 2:
+        relay_z(nz - 1)
+        relay_y(nz - 2)
+    relay_y(nz - 1)
     loads[3].wait()
     loads[4].wait()
     own.wait()
     correlate(0)
-    if nz > 2:
-        relay_z(nz - 1)
-        relay_y(nz - 2)
-    relay_y(nz - 1)
     for s in range(min(2, nz)):
         relay_x(s)
     for i in range(1, len(groups)):

time: 46.1 us -> 44.3 us (0.961)
  Pallas kernels: 44.1 us -> 42.1 us
    pallas_call x1, Pallas kernels: 44.1 us -> 42.1 us  [fused(): pl.pallas_call(functools.partial(kernel, n, m), out_shape=jax.ShapeDtypeS...]
where the time goes in v6:
time: 44.3 us; the launch traced here: 43.9 us
  Pallas kernels  42.1 us (95%)
  local copies, waits for them, and re-layouts  1.82 us (4%)
    pallas_call x1, Pallas kernels, fused(): pl.pallas_call(functools.partial(kernel, n, m), out_shape=jax.ShapeDtypeS...  42.1 us
    unnamed x1, local copies, waits for them, and re-layouts  1.82 us

profile of v6, /device:TPU:1, one launch (start us, length us, event | category | flops | bytes accessed | tf_op | source)
XLA Modules:
  0.0 43.9 jit_solution(15562058255854818460)
XLA Ops:
  0.0 42.1 %shard_map.55 = f32[16,3,2,1152]{3,2,1,0:T(2,128)} custom-call(f32[16,3,2,1152]{3,2,1,0:T(2,128)} %bitcast.4, f32[16,3,2,1152]{3,2,1,0:T(2,128)} %bitcast.5, bf16[144,288]{1,0:T(8,128)(2,1)} %w_hbm.1, bf16[512,768]{1,0:T(8,128)(2,1)} %constant.4.clone.tf_hbm, bf16[256,1536]{1,0:T(8,128)(2,1)} %constant.5.clone.ti_hbm), custom_call_target="tpu_custom_call" | custom-call | flops 2000000000 | bytes 8000000 | tf_op jit(solution)/shard_map/pallas_call | solution.py:404
  42.1 1.8 %copy.7 = f32[16,2,3,1152]{3,1,2,0:T(2,128)} copy(f32[16,2,3,1152]{3,1,2,0:T(2,128)} %bitcast.3) | data formatting | bytes 884736
